TPU v7x, 32 devices: a whole 2x2x4 slice. The times are simulated.
32 devices in a mesh: section: 2 (over core), dp: 16 (over z, y, x).
Axes of the slice: x: 2, y: 2, z: 4, core: 2. Of those that a mesh axis runs over, the one named last changes fastest.
Arguments:
- inputs: bfloat16 [4, 512, 4096], P(None, 'dp'), may hold values from -8 to 8
- cotangent: bfloat16 [4, 512, 4096], P(None, 'dp'), may hold values from -0.125 to 0.125
- weight: bfloat16 [2, 4096, 512], P('section'), may hold values from -0.09375 to 0.09375
- gain: bfloat16 [2, 4096], P('section'), may hold values from 0.099609375 to 1.8984375
Outputs:
- weight_grad: float32 [2, 4096, 512], P('section', 'dp')
- gain_grad: float32 [2, 4096], P('section', 'dp')
All inputs are finite; a program needn't handle non-finite values.
Results may differ from a plain program's by a relative error of at most 0.017.
Values may be sent and summed in bfloat16 or wider, within the bound.
A program may use at most 128 MiB of HBM per device.

v0:
```python
import jax
import jax.numpy as jnp
from jax import lax
from jax.sharding import PartitionSpec as P

EPSILON = 1e-05


def passed_along(value, axis, by):
    length = lax.axis_size(axis)
    pairs = [(i, i + by) for i in range(length) if 0 <= i + by < length]
    return lax.ppermute(value, axis, pairs)


def swapped(block, axis, bit):
    count = lax.axis_size(axis)
    route = []
    for low in range(count):
        high = low | 1 << bit
        if high != low and high < count:
            route += [(low, high), (high, low)]
    return lax.ppermute(block, axis, route)


def layer_forward(values, gain_row, weights):
    wide = values.astype(jnp.float32)
    inv_rms = lax.rsqrt(jnp.mean(wide * wide, axis=-1, keepdims=True) + EPSILON)
    normed = (wide * inv_rms * gain_row.astype(jnp.float32)).astype(jnp.bfloat16)
    hidden = jnp.dot(normed, weights, preferred_element_type=jnp.float32)
    active = jax.nn.silu(hidden).astype(jnp.bfloat16)
    back_proj = lax.dot_general(
        active, weights, (((1,), (1,)), ((), ())), preferred_element_type=jnp.float32
    )
    return ((wide + back_proj).astype(jnp.bfloat16), hidden)


def layer_backward(values, hidden, upstream, gain_row, weights):
    wide = values.astype(jnp.float32)
    gain_wide = gain_row.astype(jnp.float32)
    inv_rms = lax.rsqrt(jnp.mean(wide * wide, axis=-1, keepdims=True) + EPSILON)
    unit_rows = wide * inv_rms
    normed = (unit_rows * gain_wide).astype(jnp.bfloat16)
    logistic = jax.nn.sigmoid(hidden)
    active = jax.nn.silu(hidden).astype(jnp.bfloat16)
    grad_w = lax.dot_general(
        upstream, active, (((0,), (0,)), ((), ())), preferred_element_type=jnp.float32
    )
    d_active = jnp.dot(upstream, weights, preferred_element_type=jnp.float32)
    d_hidden = (d_active * logistic * (1.0 + hidden * (1.0 - logistic))).astype(jnp.bfloat16)
    grad_w = grad_w + lax.dot_general(
        normed, d_hidden, (((0,), (0,)), ((), ())), preferred_element_type=jnp.float32
    )
    d_normed = lax.dot_general(
        d_hidden, weights, (((1,), (1,)), ((), ())), preferred_element_type=jnp.float32
    )
    grad_g = jnp.sum(d_normed * unit_rows, axis=0)
    d_unit = d_normed * gain_wide
    d_values = inv_rms * (d_unit - unit_rows * jnp.mean(d_unit * unit_rows, axis=-1, keepdims=True))
    return ((upstream.astype(jnp.float32) + d_values).astype(jnp.bfloat16), grad_w, grad_g)


def pass_along(values, offset):
    return passed_along(values, "section", offset)


def on_device(inputs, cotangent, weight, gain):
    sections = lax.axis_size("section")
    my_section = lax.axis_index("section")
    per_pipe = inputs.shape[0] // 2
    num_steps = per_pipe + sections - 1
    levels = sections.bit_length() - 1
    own_w = weight[0]
    own_g = gain[0]
    far_w, far_g = (own_w, own_g)
    for bit_pos in range(levels):
        far_w, far_g = swapped((far_w, far_g), "section", bit_pos)
    row_count = inputs.shape[1]
    blank = jnp.zeros((row_count, inputs.shape[2]), jnp.bfloat16)
    blank_hidden = jnp.zeros((row_count, own_w.shape[1]), jnp.float32)

    def run_forward(live, values, gain_row, weights):
        return lax.cond(
            live, lambda: layer_forward(values, gain_row, weights), lambda: (blank, blank_hidden)
        )

    def forward_step(carry, step_at):
        down_in, up_in = carry
        first = jnp.minimum(step_at, per_pipe - 1)
        entering = step_at < per_pipe
        down_x = jnp.where(
            (my_section == 0) & entering,
            lax.dynamic_index_in_dim(inputs, first, 0, keepdims=False),
            down_in,
        )
        up_x = jnp.where(
            (my_section == sections - 1) & entering,
            lax.dynamic_index_in_dim(inputs, per_pipe + first, 0, keepdims=False),
            up_in,
        )
        down_m = step_at - my_section
        up_m = step_at - (sections - 1 - my_section)
        down_y, down_h = run_forward((down_m >= 0) & (down_m < per_pipe), down_x, own_g, own_w)
        up_y, up_h = run_forward((up_m >= 0) & (up_m < per_pipe), up_x, far_g, far_w)
        return ((pass_along(down_y, 1), pass_along(up_y, -1)), (down_x, down_h, up_x, up_h))

    leftover, stash = lax.scan(forward_step, (blank, blank), jnp.arange(num_steps, dtype=jnp.int32))
    stash_dx, stash_dh, stash_ux, stash_uh = stash

    def run_backward(live, values, hidden, upstream, gain_row, weights, acc_w, acc_g):

        def working():
            d_values, grad_w, grad_g = layer_backward(values, hidden, upstream, gain_row, weights)
            return (d_values, acc_w + grad_w, acc_g + grad_g)

        return lax.cond(live, working, lambda: (blank, acc_w, acc_g))

    def backward_step(carry, step_at):
        down_ct, up_ct, down_w, down_g, up_w, up_g = carry
        first = jnp.minimum(step_at, per_pipe - 1)
        entering = step_at < per_pipe
        down_c = jnp.where(
            (my_section == sections - 1) & entering,
            lax.dynamic_index_in_dim(cotangent, first, 0, keepdims=False),
            down_ct,
        )
        up_c = jnp.where(
            (my_section == 0) & entering,
            lax.dynamic_index_in_dim(cotangent, per_pipe + first, 0, keepdims=False),
            up_ct,
        )
        down_m = step_at - (sections - 1 - my_section)
        up_m = step_at - my_section
        down_at = jnp.clip(down_m + my_section, 0, num_steps - 1)
        up_at = jnp.clip(up_m + sections - 1 - my_section, 0, num_steps - 1)
        down_dx, down_w, down_g = run_backward(
            (down_m >= 0) & (down_m < per_pipe),
            lax.dynamic_index_in_dim(stash_dx, down_at, 0, keepdims=False),
            lax.dynamic_index_in_dim(stash_dh, down_at, 0, keepdims=False),
            down_c,
            own_g,
            own_w,
            down_w,
            down_g,
        )
        up_dx, up_w, up_g = run_backward(
            (up_m >= 0) & (up_m < per_pipe),
            lax.dynamic_index_in_dim(stash_ux, up_at, 0, keepdims=False),
            lax.dynamic_index_in_dim(stash_uh, up_at, 0, keepdims=False),
            up_c,
            far_g,
            far_w,
            up_w,
            up_g,
        )
        return ((pass_along(down_dx, -1), pass_along(up_dx, 1), down_w, down_g, up_w, up_g), None)

    zero_w = jnp.zeros(own_w.shape, jnp.float32)
    zero_g = jnp.zeros(own_g.shape, jnp.float32)
    final, leftover_back = lax.scan(
        backward_step,
        (blank, blank, zero_w, zero_g, zero_w, zero_g),
        jnp.arange(num_steps, dtype=jnp.int32),
    )
    down_w, down_g, up_w, up_g = (final[2], final[3], final[4], final[5])
    shard_dw, shard_uw, shard_dg, shard_ug = (
        lax.psum_scatter(down_w.astype(jnp.bfloat16), "dp", scatter_dimension=0, tiled=True).astype(
            jnp.float32
        ),
        lax.psum_scatter(up_w.astype(jnp.bfloat16), "dp", scatter_dimension=0, tiled=True).astype(
            jnp.float32
        ),
        lax.psum_scatter(down_g.astype(jnp.bfloat16), "dp", scatter_dimension=0, tiled=True).astype(
            jnp.float32
        ),
        lax.psum_scatter(up_g.astype(jnp.bfloat16), "dp", scatter_dimension=0, tiled=True).astype(
            jnp.float32
        ),
    )
    for bit_pos in range(levels):
        shard_uw, shard_ug = (
            swapped(shard_uw.astype(jnp.bfloat16), "section", bit_pos).astype(shard_uw.dtype),
            swapped(shard_ug.astype(jnp.bfloat16), "section", bit_pos).astype(shard_ug.dtype),
        )
    return ((shard_dw + shard_uw)[None], (shard_dg + shard_ug)[None])


def solution(mesh):
    placed = (
        P(None, "dp", None),
        P(None, "dp", None),
        P("section", None, None),
        P("section", None),
    )
    return jax.shard_map(
        on_device,
        mesh=mesh,
        in_specs=placed,
        out_specs=(P("section", "dp", None), P("section", "dp")),
        check_vma=False,
    )
```

profile of v0, /device:TPU:0, one launch (start us, length us, event | category | flops | bytes accessed | tf_op | source)
XLA Modules:
  0.0 400.2 jit_solution(10322242925798186615)
XLA Ops:
  8.6 5.9 %collective-permute-done.4 = bf16[4096]{0:T(1024)(128)(2,1)S(1)} collective-permute-done((bf16[4096]{0:T(1024)(128)(2,1)S(1)}, bf16[4096]{0:T(1024)(128)(2,1)S(1)}, u32[]{:S(2)}, u32[]{:S(2)}) %collective-permute-start.4) | collective-permute-done | bytes 8224 | tf_op jit(solution)/shard_map/ppermute | solution.py:22
  14.9 65.7 %while.44 = (s32[]{:T(128)}, bf16[32,4096]{1,0:T(8,128)(2,1)S(1)}, bf16[32,4096]{1,0:T(8,128)(2,1)S(1)}, bf16[3,32,4096]{2,1,0:T(8,128)(2,1)S(1)}, f32[3,32,512]...) while((s32[]{:T(128)}, bf16[32,4096]{1,0:T(8,128)(2,1)S(1)}, ...), condition=%wide.region_7.8_spmd, body=%wide.region_0.7_spmd.sunk | while | flops 539926656 | bytes 40453724 | solution.py:106
  17.5 1.2 bitcast_dynamic-update-slice_fusion.3
  19.3 1.3 collective-permute-start.1
  21.3 6.2 %conditional.8 = (bf16[32,4096]{1,0:T(8,128)(2,1)S(1)}, f32[1,32,512]{2,1,0:T(8,128)}) conditional(s32[]{:T(128)} %convert_element_type.213, () %tuple.125, (bf16[32,4096]{1,0:T(8,128)(2,1)S(1)}, bf16[4096]{0:T(1024)(128)(2,1)S(1)}, bf16[4096,512]{1,0:T(8,128)(2,1)}) %tuple.126), branch_computations={%region_1.1_spmd, %region_2.3_spmd} | conditional | flops 269832224 | bytes 26386988 | solution.py:82
  21.5 3.8 fusion.4
  25.3 2.2 fusion
  27.5 3.5 collective-permute-start
  31.1 1.6 constant_dynamic-update-slice_fusion.3
  36.4 7.5 %conditional.9 = (bf16[32,4096]{1,0:T(8,128)(2,1)S(1)}, f32[1,32,512]{2,1,0:T(8,128)}) conditional(s32[]{:T(128)} %convert_element_type.214, () %tuple.127, (bf16[32,4096]{1,0:T(8,128)(2,1)S(1)}, bf16[4096]{0:T(1024)(128)(2,1)S(1)}, bf16[4096,512]{1,0:T(8,128)(2,1)}) %tuple.128), branch_computations={%region_4.4_spmd, %region_5.6_spmd} | conditional | flops 269832224 | bytes 9609744 | solution.py:82
  36.6 3.7 fusion.14
  40.3 3.6 fusion.10
  43.8 1.3 collective-permute-start.1
  45.8 6.2 %conditional.8 = (bf16[32,4096]{1,0:T(8,128)(2,1)S(1)}, f32[1,32,512]{2,1,0:T(8,128)}) conditional(s32[]{:T(128)} %convert_element_type.213, () %tuple.125, (bf16[32,4096]{1,0:T(8,128)(2,1)S(1)}, bf16[4096]{0:T(1024)(128)(2,1)S(1)}, bf16[4096,512]{1,0:T(8,128)(2,1)}) %tuple.126), branch_computations={%region_1.1_spmd, %region_2.3_spmd} | conditional | flops 269832224 | bytes 26386988 | solution.py:82
  46.0 3.8 fusion.4
  49.8 2.2 fusion
  52.0 3.1 collective-permute-start
  55.1 1.5 constant_dynamic-update-slice_fusion.3
  60.4 7.5 %conditional.9 = (bf16[32,4096]{1,0:T(8,128)(2,1)S(1)}, f32[1,32,512]{2,1,0:T(8,128)}) conditional(s32[]{:T(128)} %convert_element_type.214, () %tuple.127, (bf16[32,4096]{1,0:T(8,128)(2,1)S(1)}, bf16[4096]{0:T(1024)(128)(2,1)S(1)}, bf16[4096,512]{1,0:T(8,128)(2,1)}) %tuple.128), branch_computations={%region_4.4_spmd, %region_5.6_spmd} | conditional | flops 269832224 | bytes 9609744 | solution.py:82
  60.6 3.7 fusion.14
  64.3 3.6 fusion.10
  67.9 1.3 collective-permute-start.1
  70.5 8.6 %collective-permute-start = (bf16[32,4096]{1,0:T(8,128)(2,1)S(1)}, bf16[32,4096]{1,0:T(8,128)(2,1)S(1)}, u32[]{:S(2)}, u32[]{:S(2)}) collective-permute-start(bf16[32,4096]{1,0:T(8,128)(2,1)S(1)} %get-tuple-element.1059), channel_id=1, source_target_pairs={{0,16},{1,17},{2,18},{3,19},{4,20},{5,21},{6,22},{7,23},{8,24},{9,... | collective-permute-start | bytes 786440 | tf_op jit(solution)/shard_map/while/body/eval_jaxpr/ppermute | solution.py:12
  79.1 1.5 constant_dynamic-update-slice_fusion.3
  80.7 4.3 %broadcast_in_dim.72 = f32[4096,512]{1,0:T(8,128)} broadcast(f32[]{:T(128)} %constant.188.clone.1), dimensions={} | broadcast | bytes 8388612 | tf_op jit(solution)/shard_map/broadcast_in_dim | solution.py:157
  85.0 4.3 %broadcast_in_dim.72.clone = f32[4096,512]{1,0:T(8,128)} broadcast(f32[]{:T(128)} %constant.188.clone.1), dimensions={} | broadcast | bytes 8388612 | tf_op jit(solution)/shard_map/broadcast_in_dim | solution.py:157
  89.4 98.9 %while.45 = (s32[]{:T(128)}, bf16[32,4096]{1,0:T(8,128)(2,1)S(1)}, bf16[32,4096]{1,0:T(8,128)(2,1)S(1)}, f32[4096,512]{1,0:T(8,128)}, f32[4096]{0:T(1024)S(1)}, ...) while((s32[]{:T(128)}, bf16[32,4096]{1,0:T(8,128)(2,1)S(1)}, ...), condition=%wide.region_19.20_spmd, body=%wide.region_8.19_spmd.sunk | while | flops 1088888832 | bytes 229855600 | solution.py:159
  92.1 15.9 %conditional.11 = (bf16[32,4096]{1,0:T(8,128)(2,1)}, f32[4096,512]{1,0:T(8,128)}, f32[4096]{0:T(1024)S(1)}) conditional(s32[]{:T(128)} %convert_element_type.216, (f32[4096,512]{1,0:T(8,128)}, f32[4096]{0:T(1024)S(1)}) %tuple.132, (pred[]{:T(512)}, pred[]{:T(512)}, s32[]{:T(128)}, bf16[4,32,4096]{2,1,0:T(8,128)(2,1)S(1)}, ...), branch_computations={%region_14.14_spmd, %region_15.18_spmd} | conditional | flops 544444416 | bytes 104965984 | solution.py:115
  92.2 3.2 fusion.51
  95.4 2.3 fusion.74
  97.9 2.5 add_add_fusion.1
  100.4 6.7 %fusion.62 = (f32[4096]{0:T(1024)S(1)}, f32[32]{0:T(128)S(1)}, f32[32,4096]{1,0:T(8,128)S(1)}) fusion(f32[32]{0:T(128)S(1)} %add_rsqrt_fusion.3, bf16[3,32,4096]{2,1,0:T(8,128)(2,1)S(1)} %get-tuple-element.687, s32[]{:T(128)S(6)} %min.26, f32[4096]{0:T(1024)S(1)} %convert_element_type.137, bf16[32,512]{1,0:T(8,128)(2,1)S(1)} %fusion.51, ...), kind=kOutput, calls=%fused_computation.88 | convolution fusion | flops 135131104 | bytes 5046532 | tf_op jit(solution)/shard_map/while/body/eval_jaxpr/cond/branch_1_fun/dot_general | solution.py:53
  108.0 1.3 collective-permute-start.3
  110.7 1.3 collective-permute-start.2
  112.0 2.3 collective-permute-done.2
  116.9 15.9 %conditional.11 = (bf16[32,4096]{1,0:T(8,128)(2,1)}, f32[4096,512]{1,0:T(8,128)}, f32[4096]{0:T(1024)S(1)}) conditional(s32[]{:T(128)} %convert_element_type.216, (f32[4096,512]{1,0:T(8,128)}, f32[4096]{0:T(1024)S(1)}) %tuple.132, (pred[]{:T(512)}, pred[]{:T(512)}, s32[]{:T(128)}, bf16[4,32,4096]{2,1,0:T(8,128)(2,1)S(1)}, ...), branch_computations={%region_14.14_spmd, %region_15.18_spmd} | conditional | flops 544444416 | bytes 104965984 | solution.py:115
  117.0 3.2 fusion.51
  120.1 2.3 fusion.74
  122.6 2.5 add_add_fusion.1
  125.1 6.7 %fusion.62 = (f32[4096]{0:T(1024)S(1)}, f32[32]{0:T(128)S(1)}, f32[32,4096]{1,0:T(8,128)S(1)}) fusion(f32[32]{0:T(128)S(1)} %add_rsqrt_fusion.3, bf16[3,32,4096]{2,1,0:T(8,128)(2,1)S(1)} %get-tuple-element.687, s32[]{:T(128)S(6)} %min.26, f32[4096]{0:T(1024)S(1)} %convert_element_type.137, bf16[32,512]{1,0:T(8,128)(2,1)S(1)} %fusion.51, ...), kind=kOutput, calls=%fused_computation.88 | convolution fusion | flops 135131104 | bytes 5046532 | tf_op jit(solution)/shard_map/while/body/eval_jaxpr/cond/branch_1_fun/dot_general | solution.py:53
  132.7 2.1 collective-permute-start.3
  135.4 11.5 %conditional.10 = (bf16[32,4096]{1,0:T(8,128)(2,1)S(1)}, f32[4096,512]{1,0:T(8,128)}, f32[4096]{0:T(1024)S(1)}) conditional(s32[]{:T(128)} %convert_element_type.215, (f32[4096,512]{1,0:T(8,128)}, f32[4096]{0:T(1024)S(1)}) %tuple.130, (pred[]{:T(512)}, pred[]{:T(512)}, s32[]{:T(128)}, bf16[4,32,4096]{2,1,0:T(8,128)(2,1)S(1)}, ...), branch_computations={%region_9.9_spmd, %region_10.13_spmd} | conditional | flops 544444416 | bytes 121743200 | solution.py:115
  135.5 3.2 fusion.21
  138.7 2.3 fusion.44
  141.2 2.5 add_add_fusion
  143.7 1.5 fusion.32
  145.4 1.5 copy-done.2
  147.7 1.3 collective-permute-start.2
  149.0 2.3 collective-permute-done.2
  154.6 17.2 %collective-permute-start.3 = (bf16[32,4096]{1,0:T(8,128)(2,1)}, bf16[32,4096]{1,0:T(8,128)(2,1)S(1)}, u32[]{:S(2)}, u32[]{:S(2)}) collective-permute-start(bf16[32,4096]{1,0:T(8,128)(2,1)} %get-tuple-element.1090), channel_id=1, source_target_pairs={{0,16},{1,17},{2,18},{3,19},{4,20},{5,21},{6,22},{7,23},{8,24},{9,... | collective-permute-start | bytes 786440 | tf_op jit(solution)/shard_map/while/body/eval_jaxpr/ppermute | solution.py:12
  172.4 11.5 %conditional.10 = (bf16[32,4096]{1,0:T(8,128)(2,1)S(1)}, f32[4096,512]{1,0:T(8,128)}, f32[4096]{0:T(1024)S(1)}) conditional(s32[]{:T(128)} %convert_element_type.215, (f32[4096,512]{1,0:T(8,128)}, f32[4096]{0:T(1024)S(1)}) %tuple.130, (pred[]{:T(512)}, pred[]{:T(512)}, s32[]{:T(128)}, bf16[4,32,4096]{2,1,0:T(8,128)(2,1)S(1)}, ...), branch_computations={%region_9.9_spmd, %region_10.13_spmd} | conditional | flops 544444416 | bytes 121743200 | solution.py:115
  172.5 3.2 fusion.21
  175.7 2.3 fusion.44
  178.2 2.5 add_add_fusion
  180.7 1.5 fusion.32
  182.4 1.5 copy-done.2
  184.6 1.3 collective-permute-start.2
  185.9 2.3 collective-permute-done.2
  188.2 5.9 %convert_element_type.153 = bf16[4096,512]{1,0:T(8,128)(2,1)} convert(f32[4096,512]{1,0:T(8,128)} %get-tuple-element.738) | non-fusion elementwise | flops 2097152 | bytes 12582912 | tf_op jit(solution)/shard_map/convert_element_type | solution.py:169
  194.2 5.9 %convert_element_type.151 = bf16[4096,512]{1,0:T(8,128)(2,1)} convert(f32[4096,512]{1,0:T(8,128)} %get-tuple-element.737) | non-fusion elementwise | flops 2097152 | bytes 12582912 | tf_op jit(solution)/shard_map/convert_element_type | solution.py:166
  200.1 91.7 %reduce-scatter.5.cloned.1.call-done = bf16[256,512]{1,0:T(8,128)(2,1)} async-done(((bf16[4096,512]{1,0:T(8,128)(2,1)}), bf16[256,512]{1,0:T(8,128)(2,1)}) %reduce-scatter.5.cloned.1.call-update) | async-done | bytes 262160 | tf_op jit(solution)/shard_map/reduce_scatter | solution.py:169
  293.1 76.0 %all-reduce.2 = (bf16[4096]{0:T(1024)(128)(2,1)S(1)}, bf16[4096]{0:T(1024)(128)(2,1)S(1)}) all-reduce(bf16[4096]{0:T(1024)(128)(2,1)S(1)} %convert_element_type.157, bf16[4096]{0:T(1024)(128)(2,1)S(1)} %convert_element_type.155), channel_id=5, replica_groups=mesh['section'=2,'dp'=16] {'dp'}, use_global_device_ids=true, to_apply=%region_23.24.clone | all-reduce | flops 8192 | bytes 32768
  370.9 20.6 %reduce-scatter.3.cloned.1.call-done = bf16[256,512]{1,0:T(8,128)(2,1)} async-done(((bf16[4096,512]{1,0:T(8,128)(2,1)}), bf16[256,512]{1,0:T(8,128)(2,1)}) %reduce-scatter.3.cloned.1.call-update) | async-done | bytes 262160 | tf_op jit(solution)/shard_map/reduce_scatter | solution.py:166
  391.6 1.8 add_bitcast_fusion
  (140 shorter events, 20.5 us)
Async XLA Ops:
  7.2 284.6 %reduce-scatter.5.cloned.1.call-start = ((), (), s32[]{:S(2)}) async-start(), calls=%async_computation.3 | async-start | bytes 4456448 | tf_op jit(solution)/shard_map/reduce_scatter | solution.py:169
  7.2 7.6 %collective-permute-start.5 = (bf16[4096,512]{1,0:T(8,128)(2,1)}, bf16[4096,512]{1,0:T(8,128)(2,1)}, u32[]{:S(2)}, u32[]{:S(2)}) collective-permute-start(bf16[4096,512]{1,0:T(8,128)(2,1)} %bitcast.107), channel_id=1, source_target_pairs={{0,16},{16,0},{1,17},{17,1},{2,18},{18,2},{3,19},{19,3},{4,20},{20... | collective-permute-start | bytes 12582920 | tf_op jit(solution)/shard_map/ppermute | solution.py:22
  8.5 6.0 %collective-permute-start.4 = (bf16[4096]{0:T(1024)(128)(2,1)S(1)}, bf16[4096]{0:T(1024)(128)(2,1)S(1)}, u32[]{:S(2)}, u32[]{:S(2)}) collective-permute-start(bf16[4096]{0:T(1024)(128)(2,1)S(1)} %reduce), channel_id=1, source_target_pairs={{0,16},{16,0},{1,17},{17,1},{2,18},{18,2},{3,19},{19,3},{4,20},{20... | collective-permute-start | bytes 24584 | tf_op jit(solution)/shard_map/ppermute | solution.py:22
  19.3 13.3 %collective-permute-start.1 = (bf16[32,4096]{1,0:T(8,128)(2,1)S(1)}, bf16[32,4096]{1,0:T(8,128)(2,1)S(1)}, u32[]{:S(2)}, u32[]{:S(2)}) collective-permute-start(bf16[32,4096]{1,0:T(8,128)(2,1)S(1)} %get-tuple-element.1061), channel_id=1, source_target_pairs={{16,0},{17,1},{18,2},{19,3},{20,4},{21,5},{22,6},{23,7},{24,8},{25... | collective-permute-start | bytes 786440 | tf_op jit(solution)/shard_map/while/body/eval_jaxpr/ppermute | solution.py:12
  21.3 4.0 %copy-start = (bf16[4096,512]{1,0:T(8,128)(2,1)S(1)}, bf16[4096,512]{1,0:T(8,128)(2,1)}, u32[]{:S(2)}) copy-start(bf16[4096,512]{1,0:T(8,128)(2,1)} %get-tuple-element.639) | copy-start | bytes 12582916 | tf_op jit(solution)/shard_map/while/body/eval_jaxpr/cond
  27.5 5.1 %collective-permute-start = (bf16[32,4096]{1,0:T(8,128)(2,1)S(1)}, bf16[32,4096]{1,0:T(8,128)(2,1)S(1)}, u32[]{:S(2)}, u32[]{:S(2)}) collective-permute-start(bf16[32,4096]{1,0:T(8,128)(2,1)S(1)} %get-tuple-element.1059), channel_id=1, source_target_pairs={{0,16},{1,17},{2,18},{3,19},{4,20},{5,21},{6,22},{7,23},{8,24},{9,... | collective-permute-start | bytes 786440 | tf_op jit(solution)/shard_map/while/body/eval_jaxpr/ppermute | solution.py:12
  43.8 12.8 %collective-permute-start.1 = (bf16[32,4096]{1,0:T(8,128)(2,1)S(1)}, bf16[32,4096]{1,0:T(8,128)(2,1)S(1)}, u32[]{:S(2)}, u32[]{:S(2)}) collective-permute-start(bf16[32,4096]{1,0:T(8,128)(2,1)S(1)} %get-tuple-element.1061), channel_id=1, source_target_pairs={{16,0},{17,1},{18,2},{19,3},{20,4},{21,5},{22,6},{23,7},{24,8},{25... | collective-permute-start | bytes 786440 | tf_op jit(solution)/shard_map/while/body/eval_jaxpr/ppermute | solution.py:12
  45.8 4.0 %copy-start = (bf16[4096,512]{1,0:T(8,128)(2,1)S(1)}, bf16[4096,512]{1,0:T(8,128)(2,1)}, u32[]{:S(2)}) copy-start(bf16[4096,512]{1,0:T(8,128)(2,1)} %get-tuple-element.639) | copy-start | bytes 12582916 | tf_op jit(solution)/shard_map/while/body/eval_jaxpr/cond
  52.0 4.6 %collective-permute-start = (bf16[32,4096]{1,0:T(8,128)(2,1)S(1)}, bf16[32,4096]{1,0:T(8,128)(2,1)S(1)}, u32[]{:S(2)}, u32[]{:S(2)}) collective-permute-start(bf16[32,4096]{1,0:T(8,128)(2,1)S(1)} %get-tuple-element.1059), channel_id=1, source_target_pairs={{0,16},{1,17},{2,18},{3,19},{4,20},{5,21},{6,22},{7,23},{8,24},{9,... | collective-permute-start | bytes 786440 | tf_op jit(solution)/shard_map/while/body/eval_jaxpr/ppermute | solution.py:12
  67.9 12.8 %collective-permute-start.1 = (bf16[32,4096]{1,0:T(8,128)(2,1)S(1)}, bf16[32,4096]{1,0:T(8,128)(2,1)S(1)}, u32[]{:S(2)}, u32[]{:S(2)}) collective-permute-start(bf16[32,4096]{1,0:T(8,128)(2,1)S(1)} %get-tuple-element.1061), channel_id=1, source_target_pairs={{16,0},{17,1},{18,2},{19,3},{20,4},{21,5},{22,6},{23,7},{24,8},{25... | collective-permute-start | bytes 786440 | tf_op jit(solution)/shard_map/while/body/eval_jaxpr/ppermute | solution.py:12
  70.5 10.2 %collective-permute-start = (bf16[32,4096]{1,0:T(8,128)(2,1)S(1)}, bf16[32,4096]{1,0:T(8,128)(2,1)S(1)}, u32[]{:S(2)}, u32[]{:S(2)}) collective-permute-start(bf16[32,4096]{1,0:T(8,128)(2,1)S(1)} %get-tuple-element.1059), channel_id=1, source_target_pairs={{0,16},{1,17},{2,18},{3,19},{4,20},{5,21},{6,22},{7,23},{8,24},{9,... | collective-permute-start | bytes 786440 | tf_op jit(solution)/shard_map/while/body/eval_jaxpr/ppermute | solution.py:12
  85.0 4.4 %copy-start.4 = (bf16[4,32,4096]{2,1,0:T(8,128)(2,1)S(1)}, bf16[4,32,4096]{2,1,0:T(8,128)(2,1)}, u32[]{:S(2)}) copy-start(bf16[4,32,4096]{2,1,0:T(8,128)(2,1)} %param.17) | copy-start | bytes 3145732
  92.2 5.7 %slice-start.2 = ((s8[8388608]{0:T(1024)(128)(4,1)}), s8[4194304]{0:T(1024)(128)(4,1)S(1)}, s32[]{:S(2)}) async-start(s8[8388608]{0:T(1024)(128)(4,1)} %bitcast.111), calls=%async_computation.6 | async-start | bytes 8388608 | tf_op jit(solution)/shard_map/while/body/eval_jaxpr/cond
  95.4 2.5 slice-start.3
  100.4 7.6 %copy-start.3 = (f32[4096,512]{1,0:T(8,128)}, f32[4096,512]{1,0:T(8,128)S(1)}, u32[]{:S(2)}) copy-start(f32[4096,512]{1,0:T(8,128)S(1)} %add_add_fusion.1) | copy-start | bytes 25165828 | tf_op jit(solution)/shard_map/while/body/eval_jaxpr/cond
  108.0 4.0 %collective-permute-start.3 = (bf16[32,4096]{1,0:T(8,128)(2,1)}, bf16[32,4096]{1,0:T(8,128)(2,1)S(1)}, u32[]{:S(2)}, u32[]{:S(2)}) collective-permute-start(bf16[32,4096]{1,0:T(8,128)(2,1)} %get-tuple-element.1090), channel_id=1, source_target_pairs={{0,16},{1,17},{2,18},{3,19},{4,20},{5,21},{6,22},{7,23},{8,24},{9,... | collective-permute-start | bytes 786440 | tf_op jit(solution)/shard_map/while/body/eval_jaxpr/ppermute | solution.py:12
  110.0 0.7 copy-start.5
  110.7 3.6 collective-permute-start.2
  116.9 5.7 %slice-start.2 = ((s8[8388608]{0:T(1024)(128)(4,1)}), s8[4194304]{0:T(1024)(128)(4,1)S(1)}, s32[]{:S(2)}) async-start(s8[8388608]{0:T(1024)(128)(4,1)} %bitcast.111), calls=%async_computation.6 | async-start | bytes 8388608 | tf_op jit(solution)/shard_map/while/body/eval_jaxpr/cond
  120.1 2.5 slice-start.3
  125.1 7.6 %copy-start.3 = (f32[4096,512]{1,0:T(8,128)}, f32[4096,512]{1,0:T(8,128)S(1)}, u32[]{:S(2)}) copy-start(f32[4096,512]{1,0:T(8,128)S(1)} %add_add_fusion.1) | copy-start | bytes 25165828 | tf_op jit(solution)/shard_map/while/body/eval_jaxpr/cond
  132.7 16.2 %collective-permute-start.3 = (bf16[32,4096]{1,0:T(8,128)(2,1)}, bf16[32,4096]{1,0:T(8,128)(2,1)S(1)}, u32[]{:S(2)}, u32[]{:S(2)}) collective-permute-start(bf16[32,4096]{1,0:T(8,128)(2,1)} %get-tuple-element.1090), channel_id=1, source_target_pairs={{0,16},{1,17},{2,18},{3,19},{4,20},{5,21},{6,22},{7,23},{8,24},{9,... | collective-permute-start | bytes 786440 | tf_op jit(solution)/shard_map/while/body/eval_jaxpr/ppermute | solution.py:12
  135.5 5.7 %slice-start = ((s8[8388608]{0:T(1024)(128)(4,1)}), s8[4194304]{0:T(1024)(128)(4,1)S(1)}, s32[]{:S(2)}) async-start(s8[8388608]{0:T(1024)(128)(4,1)} %bitcast.109), calls=%async_computation.4 | async-start | bytes 8388608 | tf_op jit(solution)/shard_map/while/body/eval_jaxpr/cond
  138.7 2.5 slice-start.1
  141.2 2.5 copy-start.1
  143.7 3.2 copy-start.2
  147.0 0.7 copy-start.5
  147.7 3.6 collective-permute-start.2
  154.6 31.4 %collective-permute-start.3 = (bf16[32,4096]{1,0:T(8,128)(2,1)}, bf16[32,4096]{1,0:T(8,128)(2,1)S(1)}, u32[]{:S(2)}, u32[]{:S(2)}) collective-permute-start(bf16[32,4096]{1,0:T(8,128)(2,1)} %get-tuple-element.1090), channel_id=1, source_target_pairs={{0,16},{1,17},{2,18},{3,19},{4,20},{5,21},{6,22},{7,23},{8,24},{9,... | collective-permute-start | bytes 786440 | tf_op jit(solution)/shard_map/while/body/eval_jaxpr/ppermute | solution.py:12
  172.5 5.7 %slice-start = ((s8[8388608]{0:T(1024)(128)(4,1)}), s8[4194304]{0:T(1024)(128)(4,1)S(1)}, s32[]{:S(2)}) async-start(s8[8388608]{0:T(1024)(128)(4,1)} %bitcast.109), calls=%async_computation.4 | async-start | bytes 8388608 | tf_op jit(solution)/shard_map/while/body/eval_jaxpr/cond
  175.7 2.5 slice-start.1
  178.2 2.5 copy-start.1
  180.7 3.2 copy-start.2
  183.9 0.7 copy-start.5
  184.6 3.6 collective-permute-start.2
  194.1 197.4 %reduce-scatter.3.cloned.1.call-start = ((), (), s32[]{:S(2)}) async-start(), calls=%async_computation.2 | async-start | bytes 4456448 | tf_op jit(solution)/shard_map/reduce_scatter | solution.py:166
  200.1 91.7 %copy-start.6 = (u32[32]{0:T(128)S(1)}, u32[32]{0:T(128)}, u32[]{:S(2)}) copy-start(u32[32]{0:T(128)} %constant.197) | copy-start | bytes 388
  291.8 99.8 %collective-permute-start.6 = (bf16[256,512]{1,0:T(8,128)(2,1)}, bf16[256,512]{1,0:T(8,128)(2,1)S(1)}, u32[]{:S(2)}, u32[]{:S(2)}) collective-permute-start(bf16[256,512]{1,0:T(8,128)(2,1)} %reduce-scatter.5.cloned.1.call-done), channel_id=1, source_target_pairs={{0,16},{16,0},{1,17},{17,1},{2,18},{18,2},{3,19},{19,3},{4,20},{20... | collective-permute-start | bytes 786440 | tf_op jit(solution)/shard_map/ppermute | solution.py:22
  369.1 1.1 collective-permute-start.7
Sparse Core Ops, SparseCore 0:
  194.3 97.4 reduce-scatter.4
  294.1 97.4 reduce-scatter.2
where the time goes:
time: 401 us; the launch traced here: 400 us
  waiting for transfers between devices  127 us (32%)
  blocking collectives  76 us (19%)
  matrix products  74.4 us (19%)
  starting transfers between devices  44.2 us (11%)
  local copies, waits for them, and re-layouts  24.8 us (6%)
  other arithmetic  22.4 us (6%)
  loops' own time  16.9 us (4%)
  between operations  14.8 us (4%)
    reduce_scatter x1, waiting for transfers between devices, on_device(): lax.psum_scatter(up_w.astype(jnp.bfloat16), 'dp', scatter_dimension=0, ti...  91.7 us
    unnamed x1, blocking collectives  76 us
    ppermute x12, starting transfers between devices, passed_along(): return lax.ppermute(value, axis, pairs)  43.5 us
    reduce_scatter x1, waiting for transfers between devices, on_device(): lax.psum_scatter(down_w.astype(jnp.bfloat16), 'dp', scatter_dimension=0,...  20.6 us
    dot_general x4, matrix products, layer_backward(): lax.dot_general(d_hidden, weights, (((1,), (1,)), ((), ())), preferred_el...  16.3 us
    dot_general x4, matrix products, layer_forward(): hidden = jnp.dot(normed, weights, preferred_element_type=jnp.float32)  15.1 us
    dot_general x4, matrix products, layer_backward(): d_active = jnp.dot(upstream, weights, preferred_element_type=jnp.float32)  12.7 us
    dot_general x4, matrix products, layer_forward(): lax.dot_general(active, weights, (((1,), (1,)), ((), ())), preferred_elem...  11.4 us
  transfers between devices with their start and end apart: 18, of which 8 were waited for; matrix products, arithmetic and copies ran while one was open for 11% of the time, Pallas kernels for 0%

commit v1 on v0

v1 whole, which is shorter than its diff:
```python
import functools

import jax
import jax.numpy as jnp
from jax import lax
from jax.experimental import pallas as pl
from jax.experimental.pallas import tpu as pltpu
from jax.sharding import PartitionSpec as P

EPSILON = 1e-05
MESH = pl.DeviceIdType.MESH
LANES = 128


def part_plan(shard, bits):
    unit = shard // 8
    near, far = [0, 1], list(range(2, bits))
    return [
        (0, 3 * unit, near + far),
        (3 * unit, 3 * unit, near[::-1] + far),
        (6 * unit, unit, far + near),
        (7 * unit, unit, far + near[::-1]),
    ]


def chunk_of(depth):
    return min(512, depth)


def relay_kernel(
    sections,
    replicas,
    x_hbm,
    ct_hbm,
    w_hbm,
    gain_ref,
    out_w,
    out_g,
    w_buf,
    v_buf,
    cn_buf,
    ad_buf,
    hid_buf,
    dact_buf,
    y_buf,
    up_buf,
    dn_buf,
    r_buf,
    part_w,
    land_w,
    part_g,
    land_g,
    x_sem,
    ct_sem,
    w_sem,
    y_send,
    y_recv,
    up_send,
    up_recv,
    rs_send,
    rs_recv,
):
    section = lax.axis_index("section")
    me = lax.axis_index("dp")
    chunks, rows, width = v_buf.shape
    depth = chunks * width
    bits = replicas.bit_length() - 1
    shard = depth // replicas
    is_first = section == 0
    is_last = section == sections - 1
    my_bit = [(me // (1 << b)) % 2 for b in range(bits)]
    partner = [me + (1 - 2 * my_bit[b]) * (1 << b) for b in range(bits)]

    def x_copy(c):
        return pltpu.make_async_copy(
            x_hbm.at[:, pl.ds(pl.multiple_of(c * width, width), width)], v_buf.at[c], x_sem.at[c]
        )

    def ct_copy(c):
        return pltpu.make_async_copy(
            ct_hbm.at[:, pl.ds(pl.multiple_of(c * width, width), width)],
            cn_buf.at[c, pl.ds(0, rows)],
            ct_sem.at[c],
        )

    def w_copy(c):
        return pltpu.make_async_copy(w_hbm.at[c], w_buf.at[c], w_sem.at[c])

    @pl.when(is_first)
    def _():
        for c in range(chunks):
            x_copy(c).start()

    @pl.when(is_last)
    def _():
        for c in range(chunks):
            ct_copy(c).start()

    for c in range(chunks):
        w_copy(c).start()

    barrier = pltpu.get_barrier_semaphore()
    for b in range(bits):
        pl.semaphore_signal(barrier, inc=1, device_id=(section, partner[b]), device_id_type=MESH)

    @pl.when(jnp.logical_not(is_first))
    def _():
        pl.semaphore_signal(barrier, inc=1, device_id=(section - 1, me), device_id_type=MESH)

    @pl.when(jnp.logical_not(is_last))
    def _():
        pl.semaphore_signal(barrier, inc=1, device_id=(section + 1, me), device_id_type=MESH)

    peers = bits + jnp.where(is_first, 0, 1) + jnp.where(is_last, 0, 1)
    pl.semaphore_wait(barrier, peers)

    def y_copy(c, to):
        return pltpu.make_async_remote_copy(
            src_ref=y_buf.at[c],
            dst_ref=v_buf.at[c],
            send_sem=y_send.at[c],
            recv_sem=y_recv.at[c],
            device_id=(to, me),
            device_id_type=MESH,
        )

    def up_copy(c, to):
        return pltpu.make_async_remote_copy(
            src_ref=up_buf.at[c],
            dst_ref=cn_buf.at[c, pl.ds(0, rows)],
            send_sem=up_send.at[c],
            recv_sem=up_recv.at[c],
            device_id=(to, me),
            device_id_type=MESH,
        )

    def each_chunk(body):
        def step(c, carry):
            body(c)
            return carry

        lax.fori_loop(0, chunks, step, 0)

    def gain_of(c):
        return gain_ref[c].astype(jnp.float32)

    def add_d_active(c):
        up = cn_buf[c, pl.ds(0, rows), :]
        dact_buf[...] += jnp.dot(up, w_buf[c], preferred_element_type=jnp.float32)

    for c in range(chunks):
        w_copy(c).wait()

    dact_buf[...] = jnp.zeros_like(dact_buf)

    @pl.when(is_last)
    def _():
        def body(c):
            ct_copy(c).wait()
            add_d_active(c)

        each_chunk(body)

    def squares(c, total):
        @pl.when(is_first)
        def _():
            x_copy(c).wait()

        @pl.when(jnp.logical_not(is_first))
        def _():
            y_copy(c, section - 1).wait_recv()

        wide = v_buf[c].astype(jnp.float32)
        return total + jnp.sum(wide * wide, axis=-1, keepdims=True)

    total = lax.fori_loop(0, chunks, squares, jnp.zeros((rows, 1), jnp.float32))
    r_buf[...] = lax.rsqrt(total / depth + EPSILON)
    hid_buf[...] = jnp.zeros_like(hid_buf)

    def project(c):
        normed = (v_buf[c].astype(jnp.float32) * r_buf[...] * gain_of(c)).astype(jnp.bfloat16)
        cn_buf[c, pl.ds(rows, rows), :] = normed
        hid_buf[...] += jnp.dot(normed, w_buf[c], preferred_element_type=jnp.float32)

    each_chunk(project)
    hidden = hid_buf[...]
    ad_buf[pl.ds(0, rows), :] = (hidden * jax.nn.sigmoid(hidden)).astype(jnp.bfloat16)

    @pl.when(jnp.logical_not(is_last))
    def _():
        def body(c):
            back = lax.dot_general(
                ad_buf[pl.ds(0, rows), :],
                w_buf[c],
                (((1,), (1,)), ((), ())),
                preferred_element_type=jnp.float32,
            )
            y_buf[c] = (v_buf[c].astype(jnp.float32) + back).astype(jnp.bfloat16)
            y_copy(c, section + 1).start()

        each_chunk(body)

        def arrived(c):
            up_copy(c, section + 1).wait_recv()
            add_d_active(c)

        each_chunk(arrived)

    hidden = hid_buf[...]
    logistic = jax.nn.sigmoid(hidden)
    ad_buf[pl.ds(rows, rows), :] = (
        dact_buf[...] * logistic * (1.0 + hidden * (1.0 - logistic))
    ).astype(jnp.bfloat16)

    per_chunk = width // shard
    plan = part_plan(shard, bits)
    gain_part = len(plan)

    def block_at(order, rel):
        index = 0
        for b, r in zip(order, rel):
            index = index + (my_bit[b] + r * (1 - 2 * my_bit[b])) * (1 << b)
        return index

    def slot_of(rel, step):
        slot = sum(1 << (bits - 1 - s) for s in range(step))
        for r in rel[step + 1 :]:
            step += 1
            slot += r << (bits - 1 - step)
        return slot

    def grad_block(j):
        c, at = j // per_chunk, j % per_chunk
        left = cn_buf[c, :, pl.ds(pl.multiple_of(at * shard, shard), shard)]
        block = lax.dot_general(
            left, ad_buf[...], (((0,), (0,)), ((), ())), preferred_element_type=jnp.float32
        )
        part_w[j] = block.astype(jnp.bfloat16)

    def views(part, j, slot):
        if part == gain_part:
            return part_g.at[j], land_g.at[slot]
        at, size, _ = plan[part]
        return part_w.at[j, pl.ds(at, size)], land_w.at[slot, pl.ds(at, size)]

    def order_of(part):
        return plan[part][2] if part < gain_part else plan[0][2]

    def hop(part, rel):
        order = order_of(part)
        step = rel.index(1)
        slot = slot_of(rel, step)
        source, target = views(part, block_at(order, rel), slot)
        return pltpu.make_async_remote_copy(
            src_ref=source,
            dst_ref=target,
            send_sem=rs_send.at[part, slot],
            recv_sem=rs_recv.at[part, slot],
            device_id=(section, partner[order[step]]),
            device_id_type=MESH,
        )

    def arrivals(part, rel, steps):
        order = order_of(part)
        own = views(part, block_at(order, rel), 0)[0]
        value = own[...].astype(jnp.float32)
        for s in range(steps):
            came = rel[:s] + (1,) + rel[s + 1 :]
            hop(part, came).wait_recv()
            value = value + views(part, 0, slot_of(came, s))[1][...].astype(jnp.float32)
        return own, value

    def combos(count):
        return [tuple((n >> (count - 1 - i)) & 1 for i in range(count)) for n in range((1 << count) - 1, -1, -1)]

    far_combos = combos(bits - 2)

    def grad_group(near):
        def step(n, carry):
            rel = list(near)
            left = (1 << (bits - 2)) - 1 - n
            for i in range(bits - 2):
                rel.append((left // (1 << (bits - 3 - i))) % 2)
            grad_block(block_at(list(range(bits)), rel))
            return carry

        lax.fori_loop(0, 1 << (bits - 2), step, 0)
        for far in far_combos:
            whole = near + far
            for part in range(gain_part):
                rel = tuple(whole[b] for b in order_of(part))
                if rel[0] == 1:
                    hop(part, rel).start()

    grad_group((1, 1))

    def through(c, total):
        dn = lax.dot_general(
            ad_buf[pl.ds(rows, rows), :],
            w_buf[c],
            (((1,), (1,)), ((), ())),
            preferred_element_type=jnp.float32,
        )
        unit = v_buf[c].astype(jnp.float32) * r_buf[...]
        both = dn * unit
        gain_sum = jnp.sum(both, axis=0, keepdims=True)
        pieces = shard // LANES
        at = lax.broadcasted_iota(jnp.int32, part_g.shape[1:], 0)
        for k in range(per_chunk):
            tile = jnp.zeros(part_g.shape[1:], jnp.float32)
            for p in range(pieces):
                piece = gain_sum[:, k * shard + p * LANES : k * shard + (p + 1) * LANES]
                tile = jnp.where(at == p, jnp.broadcast_to(piece, tile.shape), tile)
            part_g[c * per_chunk + k] = tile.astype(jnp.bfloat16)
        scaled = dn * gain_of(c)
        dn_buf[c] = scaled
        return total + jnp.sum(scaled * unit, axis=-1, keepdims=True)

    total = lax.fori_loop(0, chunks, through, jnp.zeros((rows, 1), jnp.float32))

    @pl.when(jnp.logical_not(is_first))
    def _():
        mean = total / depth

        def body(c):
            unit = v_buf[c].astype(jnp.float32) * r_buf[...]
            up = cn_buf[c, pl.ds(0, rows), :].astype(jnp.float32)
            up_buf[c] = (up + r_buf[...] * (dn_buf[c] - unit * mean)).astype(jnp.bfloat16)
            up_copy(c, section - 1).start()

        each_chunk(body)

    grad_group((1, 0))
    grad_group((0, 1))
    grad_group((0, 0))
    for rest in combos(bits - 1):
        hop(gain_part, (1,) + rest).start()

    for step in range(1, bits):
        for rest in combos(bits - 1 - step):
            rel = (0,) * step + (1,) + rest
            for part in range(gain_part + 1):
                own, value = arrivals(part, rel, step)
                own[...] = value.astype(jnp.bfloat16)
                hop(part, rel).start()
    for part in range(gain_part + 1):
        _, value = arrivals(part, (0,) * bits, bits)
        if part < gain_part:
            at, size, _ = plan[part]
            out_w[pl.ds(at, size), :] = value
        else:
            for p in range(shard // LANES):
                out_g[:, p * LANES : (p + 1) * LANES] = value[p : p + 1, :]

    for part in range(gain_part + 1):
        for step in range(bits):
            for rest in combos(bits - 1 - step):
                hop(part, (0,) * step + (1,) + rest).wait_send()

    @pl.when(jnp.logical_not(is_last))
    def _():
        for c in range(chunks):
            y_copy(c, section + 1).wait_send()

    @pl.when(jnp.logical_not(is_first))
    def _():
        for c in range(chunks):
            up_copy(c, section - 1).wait_send()


def on_device(inputs, cotangent, weight, gain):
    sections, replicas = lax.axis_size("section"), lax.axis_size("dp")
    depth, kv = weight.shape[1:]
    rows = inputs.shape[0] * inputs.shape[1]
    width = chunk_of(depth)
    chunks = depth // width
    shard = depth // replicas
    bf16, f32 = jnp.bfloat16, jnp.float32
    dma = pltpu.SemaphoreType.DMA
    parts = len(part_plan(shard, replicas.bit_length() - 1)) + 1
    vmem = pl.BlockSpec(memory_space=pltpu.VMEM)
    hbm = pl.BlockSpec(memory_space=pl.ANY)
    grad_w, grad_g = pl.pallas_call(
        functools.partial(relay_kernel, sections, replicas),
        out_shape=(
            jax.ShapeDtypeStruct((shard, kv), f32),
            jax.ShapeDtypeStruct((1, shard), f32),
        ),
        in_specs=[hbm, hbm, hbm, vmem],
        out_specs=(vmem, vmem),
        scratch_shapes=[
            pltpu.VMEM((chunks, width, kv), bf16),
            pltpu.VMEM((chunks, rows, width), bf16),
            pltpu.VMEM((chunks, 2 * rows, width), bf16),
            pltpu.VMEM((2 * rows, kv), bf16),
            pltpu.VMEM((rows, kv), f32),
            pltpu.VMEM((rows, kv), f32),
            pltpu.VMEM((chunks, rows, width), bf16),
            pltpu.VMEM((chunks, rows, width), bf16),
            pltpu.VMEM((chunks, rows, width), f32),
            pltpu.VMEM((rows, 1), f32),
            pltpu.VMEM((replicas, shard, kv), bf16),
            pltpu.VMEM((replicas - 1, shard, kv), bf16),
            pltpu.VMEM((replicas, 16, LANES), bf16),
            pltpu.VMEM((replicas - 1, 16, LANES), bf16),
            dma((chunks,)),
            dma((chunks,)),
            dma((chunks,)),
            dma((chunks,)),
            dma((chunks,)),
            dma((chunks,)),
            dma((chunks,)),
            dma((parts, replicas - 1)),
            dma((parts, replicas - 1)),
        ],
        compiler_params=pltpu.CompilerParams(
            collective_id=0, has_side_effects=True, vmem_limit_bytes=50 * 1024 * 1024
        ),
        name="relay",
    )(
        inputs.reshape(rows, depth),
        cotangent.reshape(rows, depth),
        weight.reshape(chunks, width, kv),
        gain.reshape(chunks, 1, width),
    )
    return grad_w[None], grad_g


def solution(mesh):
    placed = (
        P(None, "dp", None),
        P(None, "dp", None),
        P("section", None, None),
        P("section", None),
    )
    return jax.shard_map(
        on_device,
        mesh=mesh,
        in_specs=placed,
        out_specs=(P("section", "dp", None), P("section", "dp")),
        check_vma=False,
    )
```

time: 401 us -> 62.6 us (0.16)
  waiting for transfers between devices: 127 us -> 0 us
  blocking collectives: 76 us -> 0 us
  matrix products: 74.4 us -> 0 us
  Pallas kernels: 0 us -> 56.4 us
  starting transfers between devices: 44.2 us -> 0 us
  other arithmetic: 22.4 us -> 0 us
  local copies, waits for them, and re-layouts: 24.8 us -> 4.52 us
  loops' own time: 16.9 us -> 0 us
  between operations: 14.8 us -> 0.65 us
    reduce_scatter x2 -> x0, waiting for transfers between devices: 112 us -> none  [the longest x1 91.7 us: on_device(): lax.psum_scatter(up_w.astype(jnp.bfloat16), 'dp', scatter_dimension=0, ti...]
    unnamed x1 -> x0, blocking collectives: 76 us -> none
    dot_general x24 -> x0, matrix products: 74.4 us -> none  [the longest x4 16.3 us: layer_backward(): lax.dot_general(d_hidden, weights, (((1,), (1,)), ((), ())), preferred_el...]
    pallas_call x0 -> x1, Pallas kernels: none -> 56.4 us  [on_device(): pl.pallas_call(functools.partial(relay_kernel, sections, replicas), out_s...]
    ppermute x16 -> x0, starting transfers between devices: 44.1 us -> none  [the longest x12 43.5 us: passed_along(): return lax.ppermute(value, axis, pairs)]
    another operation x14 -> x0, loops' own time: 16.9 us -> none  [the longest x1 8.13 us: on_device(): lax.scan(backward_step, (blank, blank, zero_w, zero_g, zero_w, zero_g), j...]
    ppermute x16 -> x0, waiting for transfers between devices: 14.4 us -> none  [the longest x4 7.35 us: swapped(): return lax.ppermute(block, axis, route)]
    convert_element_type x16 -> x0, other arithmetic: 14 us -> none  [the longest x1 5.89 us: on_device(): down_w.astype(jnp.bfloat16)]
  transfers between devices with their start and end apart: 18 -> 0, of which waited for: 8 -> 0; matrix products, arithmetic and copies ran while one was open for 11% -> 0% of each run, Pallas kernels for 0% -> 0%
where the time goes in v1:
time: 62.6 us; the launch traced here: 61.6 us
  Pallas kernels  56.4 us (90%)
  local copies, waits for them, and re-layouts  4.52 us (7%)
  between operations  0.65 us (1%)
    pallas_call x1, Pallas kernels, on_device(): pl.pallas_call(functools.partial(relay_kernel, sections, replicas), out_s...  56.4 us
    unnamed x8, local copies, waits for them, and re-layouts  4.52 us

profile of v1, /device:TPU:0, one launch (start us, length us, event | category | flops | bytes accessed | tf_op | source)
XLA Modules:
  0.0 61.6 jit_solution(14017786851113989942)
XLA Ops:
  0.6 0.0 copy-start
  0.6 1.2 %copy-done = bf16[4,32,4096]{2,1,0:T(8,128)(2,1)S(1)} copy-done((bf16[4,32,4096]{2,1,0:T(8,128)(2,1)S(1)}, bf16[4,32,4096]{2,1,0:T(8,128)(2,1)}, u32[]{:S(2)}) %copy-start) | copy-done | bytes 1048600
  1.9 0.0 copy-start.1
  1.9 1.2 %copy-done.1 = bf16[4,32,4096]{2,1,0:T(8,128)(2,1)S(1)} copy-done((bf16[4,32,4096]{2,1,0:T(8,128)(2,1)S(1)}, bf16[4,32,4096]{2,1,0:T(8,128)(2,1)}, u32[]{:S(2)}) %copy-start.1) | copy-done | bytes 1048600
  3.1 0.0 copy-start.2
  3.1 0.7 %copy-done.2 = bf16[1,4096]{1,0:T(2,128)(2,1)S(1)} copy-done((bf16[1,4096]{1,0:T(2,128)(2,1)S(1)}, bf16[1,4096]{1,0:T(2,128)(2,1)}, u32[]{:S(2)}) %copy-start.2) | copy-done | bytes 8216
  3.8 56.4 %relay.1 = (f32[256,512]{1,0:T(8,128)S(1)}, f32[1,256]{1,0:T(1,128)S(1)}) custom-call(bf16[128,4096]{1,0:T(8,128)(2,1)S(1)} %bitcast.5, bf16[128,4096]{1,0:T(8,128)(2,1)S(1)} %bitcast.6, bf16[8,512,512]{2,1,0:T(8,128)(2,1)} %bitcast.9, bf16[8,1,512]{2,1,0:T(2,128)(2,1)S(1)} %bitcast.8), custom_call_target="tpu_custom_call" | custom-call | tf_op jit(solution)/shard_map/relay/pallas_call | solution.py:383
  60.2 0.8 %copy.8 = f32[1,256,512]{2,1,0:T(8,128)} copy(f32[1,256,512]{2,1,0:T(8,128)S(1)} %bitcast.7) | data formatting | bytes 1048576
  61.0 0.6 copy.9
Async XLA Ops:
  0.6 1.2 %copy-start = (bf16[4,32,4096]{2,1,0:T(8,128)(2,1)S(1)}, bf16[4,32,4096]{2,1,0:T(8,128)(2,1)}, u32[]{:S(2)}) copy-start(bf16[4,32,4096]{2,1,0:T(8,128)(2,1)} %param.4) | copy-start | bytes 3145732
  1.9 1.2 %copy-start.1 = (bf16[4,32,4096]{2,1,0:T(8,128)(2,1)S(1)}, bf16[4,32,4096]{2,1,0:T(8,128)(2,1)}, u32[]{:S(2)}) copy-start(bf16[4,32,4096]{2,1,0:T(8,128)(2,1)} %param.5) | copy-start | bytes 3145732
  3.1 0.7 %copy-start.2 = (bf16[1,4096]{1,0:T(2,128)(2,1)S(1)}, bf16[1,4096]{1,0:T(2,128)(2,1)}, u32[]{:S(2)}) copy-start(bf16[1,4096]{1,0:T(2,128)(2,1)} %param.7) | copy-start | bytes 24580

commit v2 on v1

--- a/solution.py
+++ b/solution.py
@@ -111,9 +111,6 @@
     def _():
         pl.semaphore_signal(barrier, inc=1, device_id=(section + 1, me), device_id_type=MESH)
 
-    peers = bits + jnp.where(is_first, 0, 1) + jnp.where(is_last, 0, 1)
-    pl.semaphore_wait(barrier, peers)
-
     def y_copy(c, to):
         return pltpu.make_async_remote_copy(
             src_ref=y_buf.at[c],
@@ -135,11 +132,8 @@
         )
 
     def each_chunk(body):
-        def step(c, carry):
+        for c in range(chunks):
             body(c)
-            return carry
-
-        lax.fori_loop(0, chunks, step, 0)
 
     def gain_of(c):
         return gain_ref[c].astype(jnp.float32)
@@ -173,7 +167,7 @@
         wide = v_buf[c].astype(jnp.float32)
         return total + jnp.sum(wide * wide, axis=-1, keepdims=True)
 
-    total = lax.fori_loop(0, chunks, squares, jnp.zeros((rows, 1), jnp.float32))
+    total = lax.fori_loop(0, chunks, squares, jnp.zeros((rows, 1), jnp.float32), unroll=True)
     r_buf[...] = lax.rsqrt(total / depth + EPSILON)
     hid_buf[...] = jnp.zeros_like(hid_buf)
 
@@ -185,6 +179,9 @@
     each_chunk(project)
     hidden = hid_buf[...]
     ad_buf[pl.ds(0, rows), :] = (hidden * jax.nn.sigmoid(hidden)).astype(jnp.bfloat16)
+
+    peers = bits + jnp.where(is_first, 0, 1) + jnp.where(is_last, 0, 1)
+    pl.semaphore_wait(barrier, peers)
 
     @pl.when(jnp.logical_not(is_last))
     def _():
@@ -284,7 +281,7 @@
             grad_block(block_at(list(range(bits)), rel))
             return carry
 
-        lax.fori_loop(0, 1 << (bits - 2), step, 0)
+        lax.fori_loop(0, 1 << (bits - 2), step, 0, unroll=True)
         for far in far_combos:
             whole = near + far
             for part in range(gain_part):
@@ -316,7 +313,7 @@
         dn_buf[c] = scaled
         return total + jnp.sum(scaled * unit, axis=-1, keepdims=True)
 
-    total = lax.fori_loop(0, chunks, through, jnp.zeros((rows, 1), jnp.float32))
+    total = lax.fori_loop(0, chunks, through, jnp.zeros((rows, 1), jnp.float32), unroll=True)
 
     @pl.when(jnp.logical_not(is_first))
     def _():
@@ -414,7 +411,7 @@
             dma((parts, replicas - 1)),
         ],
         compiler_params=pltpu.CompilerParams(
-            collective_id=0, has_side_effects=True, vmem_limit_bytes=50 * 1024 * 1024
+            collective_id=0, has_side_effects=True, vmem_limit_bytes=60 * 1024 * 1024
         ),
         name="relay",
     )(

time: 62.6 us -> 58 us (0.927); the launches traced: 61.6 us -> 57.7 us
  Pallas kernels: 56.4 us -> 54 us
  local copies, waits for them, and re-layouts: 4.52 us -> 3.07 us
    pallas_call x1, Pallas kernels: 56.4 us -> 54 us  [on_device(): pl.pallas_call(functools.partial(relay_kernel, sections, replicas), out_s...]
    unnamed x8 -> x2, local copies, waits for them, and re-layouts: 4.52 us -> 3.07 us
where the time goes in v2:
time: 58 us; the launch traced here: 57.7 us
  Pallas kernels  54 us (93%)
  local copies, waits for them, and re-layouts  3.07 us (5%)
  between operations  0.64 us (1%)
    pallas_call x1, Pallas kernels, on_device(): pl.pallas_call(functools.partial(relay_kernel, sections, replicas), out_s...  54 us
    unnamed x2, local copies, waits for them, and re-layouts  3.07 us

profile of v2, /device:TPU:0, one launch (start us, length us, event | category | flops | bytes accessed | tf_op | source)
XLA Modules:
  0.0 57.7 jit_solution(17116714937466307131)
XLA Ops:
  0.6 54.0 %relay.1 = (f32[256,512]{1,0:T(8,128)}, f32[1,256]{1,0:T(1,128)}) custom-call(bf16[128,4096]{1,0:T(8,128)(2,1)} %bitcast.6, bf16[128,4096]{1,0:T(8,128)(2,1)} %bitcast.7, bf16[8,512,512]{2,1,0:T(8,128)(2,1)} %bitcast.5, bf16[8,1,512]{2,1,0:T(2,128)(2,1)} %bitcast.9), custom_call_target="tpu_custom_call" | custom-call | tf_op jit(solution)/shard_map/relay/pallas_call | solution.py:380
  54.6 1.9 %copy.8 = f32[1,256,512]{2,1,0:T(8,128)} copy(f32[1,256,512]{2,1,0:T(8,128)} %bitcast.8) | data formatting | bytes 1048576
  56.5 1.2 %copy.9 = f32[1,256]{1,0:T(1,128)} copy(f32[1,256]{1,0:T(1,128)} %get-tuple-element.9) | data formatting | bytes 2048

commit v3 on v2

--- a/solution.py
+++ b/solution.py
@@ -13,14 +13,15 @@
 
 
 def part_plan(shard, bits):
-    unit = shard // 8
+    edges = [shard * e // 256 * 16 for e in (0, 5, 10, 13, 16)]
     near, far = [0, 1], list(range(2, bits))
-    return [
-        (0, 3 * unit, near + far),
-        (3 * unit, 3 * unit, near[::-1] + far),
-        (6 * unit, unit, far + near),
-        (7 * unit, unit, far + near[::-1]),
+    orders = [
+        near + far,
+        near[::-1] + far,
+        far[:1] + near + far[1:],
+        far[:1] + near[::-1] + far[1:],
     ]
+    return [(at, end - at, order) for at, end, order in zip(edges, edges[1:], orders)]
 
 
 def chunk_of(depth):
@@ -365,6 +366,11 @@
             up_copy(c, section - 1).wait_send()
 
 
+def settle_kernel(grad_w, grad_g, out_w, out_g):
+    out_w[0] = grad_w[...]
+    out_g[...] = grad_g[...]
+
+
 def on_device(inputs, cotangent, weight, gain):
     sections, replicas = lax.axis_size("section"), lax.axis_size("dp")
     depth, kv = weight.shape[1:]
@@ -420,7 +426,16 @@
         weight.reshape(chunks, width, kv),
         gain.reshape(chunks, 1, width),
     )
-    return grad_w[None], grad_g
+    return pl.pallas_call(
+        settle_kernel,
+        out_shape=(
+            jax.ShapeDtypeStruct((1, shard, kv), f32),
+            jax.ShapeDtypeStruct((1, shard), f32),
+        ),
+        in_specs=[vmem, vmem],
+        out_specs=(vmem, vmem),
+        name="settle",
+    )(grad_w, grad_g)
 
 
 def solution(mesh):

time: 58 us -> 55.7 us (0.960)
  local copies, waits for them, and re-layouts: 3.07 us -> 0 us
  Pallas kernels: 54 us -> 54.8 us
    unnamed x2 -> x0, local copies, waits for them, and re-layouts: 3.07 us -> none
    pallas_call x0 -> x1, Pallas kernels: none -> 1.87 us  [on_device(): pl.pallas_call(settle_kernel, out_shape=(jax.ShapeDtypeStruct((1, shard,...]
    pallas_call x1, Pallas kernels: 54 us -> 52.9 us  [on_device(): pl.pallas_call(functools.partial(relay_kernel, sections, replicas), out_s...]
where the time goes in v3:
time: 55.7 us; the launch traced here: 55.5 us
  Pallas kernels  54.8 us (98%)
  between operations  0.64 us (1%)
    pallas_call x1, Pallas kernels, on_device(): pl.pallas_call(functools.partial(relay_kernel, sections, replicas), out_s...  52.9 us
    pallas_call x1, Pallas kernels, on_device(): pl.pallas_call(settle_kernel, out_shape=(jax.ShapeDtypeStruct((1, shard,...  1.87 us

profile of v3, /device:TPU:0, one launch (start us, length us, event | category | flops | bytes accessed | tf_op | source)
XLA Modules:
  0.0 55.5 jit_solution(12789628141623103762)
XLA Ops:
  0.6 52.9 %relay.1 = (f32[256,512]{1,0:T(8,128)}, f32[1,256]{1,0:T(1,128)}) custom-call(bf16[128,4096]{1,0:T(8,128)(2,1)} %bitcast.5, bf16[128,4096]{1,0:T(8,128)(2,1)} %bitcast.6, bf16[8,512,512]{2,1,0:T(8,128)(2,1)} %bitcast.4, bf16[8,1,512]{2,1,0:T(2,128)(2,1)} %bitcast.7), custom_call_target="tpu_custom_call" | custom-call | tf_op jit(solution)/shard_map/relay/pallas_call | solution.py:386
  53.6 1.9 %settle.1 = (f32[1,256,512]{2,1,0:T(8,128)}, f32[1,256]{1,0:T(1,128)}) custom-call(f32[256,512]{1,0:T(8,128)} %get-tuple-element.4.grad_w, f32[1,256]{1,0:T(1,128)} %get-tuple-element.5.grad_g), custom_call_target="tpu_custom_call" | custom-call | tf_op jit(solution)/shard_map/settle/pallas_call | solution.py:429
